TPU v7x, 32 devices: a whole 2x2x4 slice. The times are simulated.
32 devices in a mesh: kv: 4 (over y, core), blk: 8 (over z, x).
Axes of the slice: x: 2, y: 2, z: 4, core: 2. Of those that a mesh axis runs over, the one named last changes fastest.
Arguments:
- queries: bfloat16 [256, 8192], P('blk', 'kv'), may hold values from -40 to 40
- draft_token_keys: bfloat16 [256, 1024], P('blk', 'kv'), may hold values from -15 to 15
- draft_token_values: bfloat16 [256, 1024], P('blk', 'kv'), may hold values from -6 to 6
- cached_key_vectors: bfloat16 [4, 4096, 1024], P(None, 'blk', 'kv'), may hold values from -40 to 40
- cached_value_vectors: bfloat16 [4, 4096, 1024], P(None, 'blk', 'kv'), may hold values from -6 to 6
- out_weight: bfloat16 [8192, 8192], P('kv', 'blk'), may hold values from -0.5 to 0.5
- lengths: int32 [4], replicated, may hold values from 256 to 4088, as said below
- parents: int32 [4, 64], replicated, may hold values from 0 to 62, as said below
- accepted_nodes: int32 [4, 8], replicated, may hold values from 0 to 62, as said below
- accepted_count: int32 [4], replicated, may hold values from 1 to 8, as said below
Outputs:
- projected: bfloat16 [256, 8192], P('kv', 'blk')
- new_cache_keys: bfloat16 [4, 4096, 1024], P(None, 'blk', 'kv')
- new_cache_values: bfloat16 [4, 4096, 1024], P(None, 'blk', 'kv')
Inputs may be any that keep to these rules, and one draw needn't show every extreme that they name: `lengths`: some request has exactly 4088, some exactly 256. parents[r, 0] = 0 and parents[r, i] < i for i >= 1. accepted_nodes[r, 0] = 0 and accepted_nodes[r, k] is a child of accepted_nodes[r, k - 1] in request r's tree; only the first accepted_count[r] entries are used. `accepted_count`: some request has exactly 8, some exactly 1.
All inputs are finite; a program needn't handle non-finite values.
Results may differ from a plain program's by a relative error of at most 0.0055.
Values may be sent and summed in bfloat16 or wider, within the bound.
A program may use at most 64 MiB of HBM per device.

v0:
```python
import math

import jax
import jax.numpy as jnp
from jax import lax
from jax.sharding import PartitionSpec as P

HEAD_SIZE = 128
TREE_TOKENS = 64
ACC = 8


NEG_FLOOR = -1e30


def ancestors(parent_rows):
    node_ids = jnp.arange(TREE_TOKENS, dtype=jnp.int32)
    parent_link = (
        (parent_rows[:, :, None] == node_ids[None, None, :]) & (node_ids[None, :, None] >= 1)
    ).astype(jnp.float32)
    reachable = jnp.eye(TREE_TOKENS, dtype=jnp.float32)[None] + parent_link
    for doubling in range((TREE_TOKENS - 1).bit_length()):
        reachable = jnp.minimum(
            reachable
            + jnp.einsum("rij,rjk->rik", reachable, reachable, precision=lax.Precision.HIGHEST),
            1.0,
        )
    return reachable


def partial_softmax(query_vectors, key_rows, value_rows, usable, score_scale):
    scores = (
        jnp.einsum(
            "rtkgh,rbpkh->brkgtp", query_vectors, key_rows, preferred_element_type=jnp.float32
        )
        * score_scale
    )
    scores = jnp.where(usable, scores, NEG_FLOOR)
    peak_score = jnp.max(scores, axis=-1)
    weights = jnp.where(usable, jnp.exp(scores - peak_score[..., None]), 0.0)
    weight_sum = jnp.sum(weights, axis=-1)
    weighted = jnp.einsum(
        "brkgtp,rbpkh->brtkgh",
        weights.astype(jnp.bfloat16),
        value_rows,
        preferred_element_type=jnp.float32,
    )
    block_count, req_count, kv_count, query_group_width, row_count = peak_score.shape
    weighted = weighted.reshape(
        block_count, req_count * row_count, kv_count * query_group_width * value_rows.shape[-1]
    )
    peak_score = peak_score.transpose(0, 1, 4, 2, 3).reshape(
        block_count, req_count * row_count, kv_count * query_group_width
    )
    weight_sum = weight_sum.transpose(0, 1, 4, 2, 3).reshape(
        block_count, req_count * row_count, kv_count * query_group_width
    )
    return (weighted, peak_score, weight_sum)


def merge_parts(cache_part, draft_part, head_dim):
    cache_out, cache_peak, cache_sum = cache_part
    draft_out, draft_peak, draft_sum = draft_part
    cache_out = cache_out.astype(jnp.float32)
    overall = jnp.maximum(jnp.max(cache_peak, axis=0), draft_peak[0])
    cache_factor = jnp.exp(cache_peak - overall[None])
    draft_factor = jnp.exp(draft_peak[0] - overall)
    denominator = jnp.sum(cache_factor * cache_sum, axis=0) + draft_factor * draft_sum[0]
    block_count, row_count, head_count = cache_peak.shape
    numerator = jnp.sum(
        cache_factor[..., None] * cache_out.reshape(block_count, row_count, head_count, head_dim),
        axis=0,
    )
    numerator = numerator + draft_factor[..., None] * draft_out[0].reshape(
        row_count, head_count, head_dim
    )
    return (
        (numerator / denominator[..., None])
        .reshape(row_count, head_count * head_dim)
        .astype(jnp.bfloat16)
    )


def place_rows(sources, slot_index, written, cache_rows):
    slot_ids = jnp.arange(sources.shape[1], dtype=jnp.int32)
    selector = ((slot_index[:, :, None] == slot_ids[None, None, :]) & written[:, :, None]).astype(
        jnp.bfloat16
    )
    placed = jnp.einsum(
        "rps,rsc->rpc", selector, sources, preferred_element_type=jnp.float32
    ).astype(jnp.bfloat16)
    return jnp.where(written[:, :, None], placed, cache_rows)


def on_device(
    queries,
    draft_token_keys,
    draft_token_values,
    cached_key_vectors,
    cached_value_vectors,
    out_weight,
    lengths,
    parents,
    accepted_nodes,
    accepted_count,
):
    block_count = lax.axis_size("blk")
    my_block = lax.axis_index("blk")
    rows_dev, width_q = queries.shape
    requests = lengths.shape[0]
    cache_width = cached_key_vectors.shape[2]
    kv_local = cache_width // HEAD_SIZE
    query_group_width = width_q // (kv_local * HEAD_SIZE)
    block_len = cached_key_vectors.shape[1]
    score_scale = 1.0 / math.sqrt(HEAD_SIZE)
    leading_row = my_block * rows_dev
    my_request = leading_row // TREE_TOKENS
    node_start = leading_row - my_request * TREE_TOKENS
    local_queries = queries.reshape(1, rows_dev, kv_local, query_group_width, HEAD_SIZE)
    gathered_keys, gathered_values = (
        lax.all_gather(draft_token_keys, "blk", axis=0, tiled=True),
        lax.all_gather(draft_token_values, "blk", axis=0, tiled=True),
    )
    tree_keys = lax.dynamic_slice_in_dim(
        gathered_keys, my_request * TREE_TOKENS, TREE_TOKENS, 0
    ).reshape(1, 1, TREE_TOKENS, kv_local, HEAD_SIZE)
    tree_values = lax.dynamic_slice_in_dim(
        gathered_values, my_request * TREE_TOKENS, TREE_TOKENS, 0
    ).reshape(1, 1, TREE_TOKENS, kv_local, HEAD_SIZE)
    reachable = ancestors(lax.dynamic_slice_in_dim(parents, my_request, 1, 0))
    own_reach = lax.dynamic_slice_in_dim(reachable, node_start, rows_dev, 1)
    draft_usable = (own_reach > 0.5)[None, :, None, None, :, :]
    draft_part = partial_softmax(local_queries, tree_keys, tree_values, draft_usable, score_scale)
    every_query = lax.all_gather(queries, "blk", axis=0, tiled=True)
    all_queries = every_query.reshape(requests, TREE_TOKENS, kv_local, query_group_width, HEAD_SIZE)
    positions = my_block * block_len + jnp.arange(block_len, dtype=jnp.int32)
    usable = (positions[None, :] < lengths[:, None])[None, :, None, None, None, :]
    local_out, local_peak, local_sum = partial_softmax(
        all_queries,
        cached_key_vectors.reshape(requests, 1, block_len, kv_local, HEAD_SIZE),
        cached_value_vectors.reshape(requests, 1, block_len, kv_local, HEAD_SIZE),
        usable,
        score_scale,
    )
    moved_out = lax.all_to_all(
        local_out[0].astype(jnp.bfloat16), "blk", split_axis=0, concat_axis=0, tiled=True
    )
    moved_peak, moved_sum = (
        lax.all_to_all(local_peak[0], "blk", split_axis=0, concat_axis=0, tiled=True),
        lax.all_to_all(local_sum[0], "blk", split_axis=0, concat_axis=0, tiled=True),
    )
    cache_part = (
        moved_out.reshape(block_count, rows_dev, -1),
        moved_peak.reshape(block_count, rows_dev, -1),
        moved_sum.reshape(block_count, rows_dev, -1),
    )
    attention = merge_parts(cache_part, draft_part, HEAD_SIZE)
    every_row = lax.all_gather(attention, "blk", axis=0, tiled=True)
    projected = lax.psum_scatter(
        jnp.dot(every_row, out_weight, preferred_element_type=jnp.float32),
        "kv",
        scatter_dimension=0,
        tiled=True,
    ).astype(jnp.bfloat16)
    positions_here = my_block * block_len + jnp.arange(block_len, dtype=jnp.int32)
    offset = positions_here[None, :] - lengths[:, None]
    written = (offset >= 0) & (offset < accepted_count[:, None])
    slot_match = offset[:, :, None] == jnp.arange(ACC, dtype=jnp.int32)[None, None, :]
    node_ids = jnp.sum(jnp.where(slot_match, accepted_nodes[:, None, :], 0), axis=-1)
    new_cache_keys = place_rows(
        gathered_keys.reshape(requests, TREE_TOKENS, cache_width),
        node_ids,
        written,
        cached_key_vectors,
    )
    new_cache_values = place_rows(
        gathered_values.reshape(requests, TREE_TOKENS, cache_width),
        node_ids,
        written,
        cached_value_vectors,
    )
    return (projected, new_cache_keys, new_cache_values)


def solution(mesh):
    return jax.shard_map(
        on_device,
        mesh=mesh,
        in_specs=(
            P("blk", "kv"),
            P("blk", "kv"),
            P("blk", "kv"),
            P(None, "blk", "kv"),
            P(None, "blk", "kv"),
            P("kv", "blk"),
            P(),
            P(),
            P(),
            P(),
        ),
        out_specs=(P("kv", "blk"), P(None, "blk", "kv"), P(None, "blk", "kv")),
        check_vma=False,
    )
```

profile of v0, /device:TPU:1, one launch (start us, length us, event | category | flops | bytes accessed | tf_op | source)
XLA Modules:
  0.0 210.8 jit_solution(3671896293867023256)
XLA Ops:
  7.9 26.0 %all_gather.13 = bf16[256,256]{1,0:T(8,128)(2,1)S(1)} all-gather(bf16[32,256]{1,0:T(8,128)(2,1)} %param.11), channel_id=1, replica_groups=mesh['kv'=4,'blk'=8] {'blk'}, dimensions={0}, use_global_device_ids=true | all-gather | bytes 147456 | tf_op jit(solution)/shard_map/all_gather | solution.py:121
  33.9 24.9 %all_gather.14 = bf16[256,256]{1,0:T(8,128)(2,1)S(1)} all-gather(bf16[32,256]{1,0:T(8,128)(2,1)} %param.12), channel_id=1, replica_groups=mesh['kv'=4,'blk'=8] {'blk'}, dimensions={0}, use_global_device_ids=true | all-gather | bytes 147456 | tf_op jit(solution)/shard_map/all_gather | solution.py:122
  59.5 0.9 copy.74
  60.4 1.3 reshape.448
  61.8 1.3 reshape.453
  63.2 0.8 compare_and_fusion
  64.9 1.5 copy.73
  66.3 4.6 %bitcast_reduce_fusion = (f32[4,2,8,64]{3,2,1,0:T(8,128)S(1)}, f32[4,2,512,64,8]{2,3,4,1,0:T(8,128)}) fusion(pred[4,512]{1,0:T(4,128)(4,1)S(1)} %get-tuple-element.8, bf16[4,64,2,8,128]{4,3,2,1,0:T(8,128)(2,1)S(1)} %bitcast.154, bf16[4,512,2,128,1]{3,2,1,0,4:T(2,128)(2,1)S(1)} %bitcast.153), kind=kOutput, calls=%fused_computation.1 | convolution fusion | flops 543158272 | bytes 10504192 | tf_op jit(solution)/shard_map/rtkgh,rbpkh->brkgtp/dot_general | solution.py:33
  71.8 4.9 %all-to-all-start = ((f32[8,1,512]{2,1,0:T(1,128)}), f32[8,1,512]{2,1,0:T(1,128)S(1)}, u32[]{:S(2)}, u32[]{:S(2)}) async-start(f32[8,1,512]{2,1,0:T(1,128)} %reshape.462), calls=%async_computation | async-start | bytes 32768 | tf_op jit(solution)/shard_map/all_to_all | solution.py:149
  76.6 4.7 %fusion.2 = f32[4,2,8,64]{3,2,1,0:T(8,128)S(1)} fusion(f32[4,2,512,64,8]{2,3,4,1,0:T(8,128)} %get-tuple-element.10, f32[4,2,8,64]{3,2,1,0:T(8,128)S(1)} %get-tuple-element.9, pred[4,512]{1,0:T(4,128)(4,1)S(1)} %get-tuple-element.8), kind=kLoop, calls=%fused_computation.5 | loop fusion | flops 10481664 | bytes 8423424 | tf_op jit(solution)/shard_map/reduce_sum | solution.py:41
  82.1 5.4 %all-to-all-start.2 = ((f32[8,1,512]{2,1,0:T(1,128)}), f32[8,1,512]{2,1,0:T(1,128)S(1)}, u32[]{:S(2)}, u32[]{:S(2)}) async-start(f32[8,1,512]{2,1,0:T(1,128)} %reshape.464), calls=%async_computation.2 | async-start | bytes 32768 | tf_op jit(solution)/shard_map/all_to_all | solution.py:150
  87.6 5.4 %fusion.14 = bf16[1,4,64,2,8,128]{5,2,4,3,1,0:T(8,128)(2,1)S(1)} fusion(f32[4,2,512,64,8]{2,3,4,1,0:T(8,128)} %get-tuple-element.10, f32[4,2,8,64]{3,2,1,0:T(8,128)S(1)} %get-tuple-element.9, pred[4,512]{1,0:T(4,128)(4,1)S(1)} %get-tuple-element.8, bf16[4,512,2,128,1]{3,2,1,0,4:T(2,128)(2,1)S(1)} %bitcast.152), kind=kOutput, calls=%fused_computation.17 | convolution fusion | flops 547880960 | bytes 10504192 | tf_op jit(solution)/shard_map/brkgtp,rbpkh->brtkgh/dot_general | solution.py:42
  93.7 1.3 convert_element_type.101
  95.0 5.4 %all-to-all-start.1 = ((bf16[8,32,2048]{2,1,0:T(8,128)(2,1)}), bf16[8,32,2048]{2,1,0:T(8,128)(2,1)}, u32[]{:S(2)}, u32[]{:S(2)}) async-start(bf16[8,32,2048]{2,1,0:T(8,128)(2,1)} %convert_element_type.101), calls=%async_computation.1 | async-start | bytes 2097152 | tf_op jit(solution)/shard_map/all_to_all | solution.py:145
  101.6 0.9 fusion.37
  106.5 2.0 mul.76
  108.5 1.8 mul.77
  110.3 1.3 fusion.51
  111.7 1.4 copy.55
  113.0 1.4 copy.60
  114.4 1.2 all-to-all-done.1
  115.6 1.6 multiply_reduce_fusion
  117.2 0.9 mul.79
  118.1 0.8 div.22
  119.0 0.9 fusion.31
  119.9 53.2 %all-gather.5.cloned.1.call-done = bf16[256,2048]{1,0:T(8,128)(2,1)} async-done(((bf16[32,2048]{1,0:T(8,128)(2,1)}), bf16[256,2048]{1,0:T(8,128)(2,1)}) %all-gather.5.cloned.1.call-update) | async-done | bytes 1048592 | tf_op jit(solution)/shard_map/all_gather | solution.py:158
  173.1 4.8 %fusion.61 = f32[256,1024]{1,0:T(8,128)} fusion(bf16[256,2048]{1,0:T(8,128)(2,1)} %all-gather.5.cloned.1.call-done, bf16[2048,1024]{1,0:T(8,128)(2,1)} %param.15), kind=kOutput, calls=%fused_computation.92 | convolution fusion | flops 1073741824 | bytes 6291456 | tf_op jit(solution)/shard_map/dot_general | solution.py:160
  178.6 0.8 select_reduce_fusion
  179.4 1.6 fusion.12
  181.0 1.6 fusion.13
  182.6 20.0 %reduce-scatter.2.cloned.1.call-done = f32[64,1024]{1,0:T(8,128)} async-done(((f32[256,1024]{1,0:T(8,128)}), f32[64,1024]{1,0:T(8,128)}) %reduce-scatter.2.cloned.1.call-update) | async-done | bytes 262160 | tf_op jit(solution)/shard_map/reduce_scatter | solution.py:159
  202.6 1.6 convert_element_type.105
  (58 shorter events, 10.6 us)
Async XLA Ops:
  7.2 56.0 %copy-start = (s32[4,64]{1,0:T(4,128)S(1)}, s32[4,64]{1,0:T(4,128)}, u32[]{:S(2)}) copy-start(s32[4,64]{1,0:T(4,128)} %param.17) | copy-start | bytes 3076
  7.2 57.7 %all-gather.3.cloned.1.call-start = ((), (), s32[]{:S(2)}) async-start(), calls=%async_computation.4 | async-start | bytes 1179648 | tf_op jit(solution)/shard_map/all_gather | solution.py:134
  58.8 0.7 copy-start.3
  63.2 7.8 %copy-start.5 = (s32[512]{0:T(512)}, s32[512]{0:T(512)S(1)}, u32[]{:S(2)}) copy-start(s32[512]{0:T(512)S(1)} %iota_add_fusion) | copy-start | bytes 6148
  71.8 10.4 %all-to-all-start = ((f32[8,1,512]{2,1,0:T(1,128)}), f32[8,1,512]{2,1,0:T(1,128)S(1)}, u32[]{:S(2)}, u32[]{:S(2)}) async-start(f32[8,1,512]{2,1,0:T(1,128)} %reshape.462), calls=%async_computation | async-start | bytes 32768 | tf_op jit(solution)/shard_map/all_to_all | solution.py:149
  82.1 12.8 %all-to-all-start.2 = ((f32[8,1,512]{2,1,0:T(1,128)}), f32[8,1,512]{2,1,0:T(1,128)S(1)}, u32[]{:S(2)}, u32[]{:S(2)}) async-start(f32[8,1,512]{2,1,0:T(1,128)} %reshape.464), calls=%async_computation.2 | async-start | bytes 32768 | tf_op jit(solution)/shard_map/all_to_all | solution.py:150
  95.0 20.6 %all-to-all-start.1 = ((bf16[8,32,2048]{2,1,0:T(8,128)(2,1)}), bf16[8,32,2048]{2,1,0:T(8,128)(2,1)}, u32[]{:S(2)}, u32[]{:S(2)}) async-start(bf16[8,32,2048]{2,1,0:T(8,128)(2,1)} %convert_element_type.101), calls=%async_computation.1 | async-start | bytes 2097152 | tf_op jit(solution)/shard_map/all_to_all | solution.py:145
  100.4 72.7 %all-gather.5.cloned.1.call-start = ((), (), s32[]{:S(2)}) async-start(), calls=%async_computation.5 | async-start | bytes 1179648 | tf_op jit(solution)/shard_map/all_gather | solution.py:158
  108.5 70.9 %copy-start.1 = (bf16[4,512,256]{2,1,0:T(8,128)(2,1)S(1)}, bf16[4,512,256]{2,1,0:T(8,128)(2,1)}, u32[]{:S(2)}) copy-start(bf16[4,512,256]{2,1,0:T(8,128)(2,1)} %param.13) | copy-start | bytes 3145732
  117.2 63.8 %copy-start.2 = (bf16[4,512,256]{2,1,0:T(8,128)(2,1)S(1)}, bf16[4,512,256]{2,1,0:T(8,128)(2,1)}, u32[]{:S(2)}) copy-start(bf16[4,512,256]{2,1,0:T(8,128)(2,1)} %param.14) | copy-start | bytes 3145732
  117.2 63.8 %copy-start.4 = (bf16[256,256]{1,0:T(8,128)(2,1)S(1)}, bf16[256,256]{1,0:T(8,128)(2,1)}, u32[]{:S(2)}) copy-start(bf16[256,256]{1,0:T(8,128)(2,1)} %copy-done.3) | copy-start | bytes 393220
  119.9 82.8 %reduce-scatter.2.cloned.1.call-start = ((), (), s32[]{:S(2)}) async-start(), calls=%async_computation.6 | async-start | bytes 1310720 | tf_op jit(solution)/shard_map/reduce_scatter | solution.py:159
Sparse Core Ops, SparseCore 0:
  10.1 41.5 all-gather.2
  120.0 53.0 all-gather.4
  178.0 24.6 reduce-scatter.1
where the time goes:
time: 212 us; the launch traced here: 211 us
  waiting for transfers between devices  75.1 us (35%)
  blocking collectives  50.8 us (24%)
  matrix products  19.6 us (9%)
  local copies, waits for them, and re-layouts  18.6 us (9%)
  other arithmetic  16.7 us (8%)
  starting transfers between devices  15.9 us (8%)
  between operations  14.1 us (7%)
    all_gather x1, waiting for transfers between devices, on_device(): every_row = lax.all_gather(attention, 'blk', axis=0, tiled=True)  53.2 us
    all_gather x1, blocking collectives, on_device(): lax.all_gather(draft_token_keys, 'blk', axis=0, tiled=True)  26 us
    all_gather x1, blocking collectives, on_device(): lax.all_gather(draft_token_values, 'blk', axis=0, tiled=True)  24.9 us
    reduce_scatter x1, waiting for transfers between devices, on_device(): lax.psum_scatter(jnp.dot(every_row, out_weight, preferred_element_type=jn...  20 us
    dot_general x2, matrix products, partial_softmax(): jnp.einsum('brkgtp,rbpkh->brtkgh', weights.astype(jnp.bfloat16), value_ro...  5.68 us
    reduce_sum x2, other arithmetic, partial_softmax(): weight_sum = jnp.sum(weights, axis=-1)  5.52 us
    all_to_all x1, starting transfers between devices, on_device(): lax.all_to_all(local_out[0].astype(jnp.bfloat16), 'blk', split_axis=0, co...  5.44 us
    all_to_all x1, starting transfers between devices, on_device(): lax.all_to_all(local_sum[0], 'blk', split_axis=0, concat_axis=0, tiled=True)  5.43 us
  transfers between devices with their start and end apart: 6, of which 3 were waited for; matrix products, arithmetic and copies ran while one was open for 17% of the time, Pallas kernels for 0%

commit v1 on v0

--- a/solution.py
+++ b/solution.py
@@ -1,8 +1,11 @@
+import functools
 import math
 
 import jax
 import jax.numpy as jnp
 from jax import lax
+from jax.experimental import pallas as pl
+from jax.experimental.pallas import tpu as pltpu
 from jax.sharding import PartitionSpec as P
 
 HEAD_SIZE = 128
@@ -182,9 +185,469 @@
     return (projected, new_cache_keys, new_cache_values)
 
 
+LOG2E = 1.4426950408889634
+MESH_ID = pl.DeviceIdType.MESH
+ABSENT = -1e20
+
+
+def fused_kernel(
+    z_count,
+    kv_count,
+    len_ref,
+    count_ref,
+    nodes_ref,
+    parents_ref,
+    q_ref,
+    dk_ref,
+    dv_ref,
+    key_hbm,
+    value_hbm,
+    weight_hbm,
+    out_ref,
+    new_key_hbm,
+    new_value_hbm,
+    gq,
+    keys,
+    values,
+    weight,
+    own_o,
+    own_st,
+    xs_o,
+    xs_st,
+    xr_o,
+    xr_st,
+    zs_o,
+    zs_st,
+    zr_o,
+    zr_st,
+    ag,
+    rs_send,
+    rs_recv,
+    local_sem,
+    gz_send,
+    gz_recv,
+    gx_send,
+    gx_recv,
+    x_send,
+    x_recv,
+    z_send,
+    z_recv,
+    az_send,
+    az_recv,
+    ax_send,
+    ax_recv,
+    r_send,
+    r_recv,
+):
+    kv = lax.axis_index("kv")
+    blk = lax.axis_index("blk")
+    z = blk // 2
+    x = blk % 2
+    other = 1 - x
+    partner = (kv, z * 2 + other)
+    rows, width_q = q_ref.shape
+    width_kv = dk_ref.shape[1]
+    groups = width_kv // HEAD_SIZE
+    heads = width_q // width_kv
+    cols = rows * heads
+    requests, block_len, _ = keys.shape
+    scale = LOG2E / math.sqrt(HEAD_SIZE)
+
+    def z_at(step):
+        return lax.rem(z + step, z_count)
+
+    def z_back(step):
+        return lax.rem(z + z_count - step, z_count)
+
+    load_keys = pltpu.make_async_copy(key_hbm, keys, local_sem.at[0])
+    load_values = pltpu.make_async_copy(value_hbm, values, local_sem.at[1])
+    load_weight = pltpu.make_async_copy(weight_hbm, weight, local_sem.at[2])
+    load_keys.start()
+    load_values.start()
+    load_weight.start()
+
+    gq[blk, :, 0:width_q] = q_ref[...]
+    gq[blk, :, width_q : width_q + width_kv] = dk_ref[...]
+    gq[blk, :, width_q + width_kv :] = dv_ref[...]
+
+    barrier = pltpu.get_barrier_semaphore()
+    pl.semaphore_signal(barrier, inc=1, device_id=partner, device_id_type=MESH_ID)
+    for step in range(1, z_count):
+        pl.semaphore_signal(
+            barrier, inc=1, device_id=(kv, z_at(step) * 2 + x), device_id_type=MESH_ID
+        )
+    for step in range(1, kv_count):
+        pl.semaphore_signal(
+            barrier, inc=1, device_id=(lax.rem(kv + step, kv_count), blk), device_id_type=MESH_ID
+        )
+    pl.semaphore_wait(barrier, z_count + kv_count - 1)
+
+    def remote(src, dst, send, recv, device):
+        return pltpu.make_async_remote_copy(
+            src_ref=src,
+            dst_ref=dst,
+            send_sem=send,
+            recv_sem=recv,
+            device_id=device,
+            device_id_type=MESH_ID,
+        )
+
+    def gather_start(buf, zs, zr, xs, xr):
+        here = buf.at[blk]
+        remote(here, here, xs.at[0], xr.at[0], partner).start()
+        for step in range(1, z_count):
+            remote(here, here, zs.at[step], zr.at[step], (kv, z_at(step) * 2 + x)).start()
+
+    def gather_forward(buf, step, zs, zr, xs, xr):
+        slot = buf.at[z_back(step) * 2 + x]
+        remote(slot, slot, zs.at[step], zr.at[step], partner).wait_recv()
+        remote(slot, slot, xs.at[step], xr.at[step], partner).start()
+
+    def gather_wait(buf, step, xs, xr):
+        slot = buf.at[z_back(step) * 2 + other]
+        remote(slot, slot, xs.at[step], xr.at[step], partner).wait_recv()
+
+    def gather_drain(buf, zs, zr, xs, xr):
+        here = buf.at[blk]
+        for step in range(z_count):
+            remote(here, here, xs.at[step], xr.at[step], partner).wait_send()
+            if step:
+                remote(here, here, zs.at[step], zr.at[step], partner).wait_send()
+
+    gather_start(gq, gz_send, gz_recv, gx_send, gx_recv)
+
+    node_row = lax.broadcasted_iota(jnp.int32, (TREE_TOKENS, TREE_TOKENS), 0)
+    node_col = lax.broadcasted_iota(jnp.int32, (TREE_TOKENS, TREE_TOKENS), 1)
+    parent_row = parents_ref[pl.ds(z, 1), :]
+    reach = jnp.where(
+        (node_row == node_col) | ((parent_row == node_row) & (node_col >= 1)), 1.0, 0.0
+    )
+    for _ in range((TREE_TOKENS - 1).bit_length()):
+        half = reach.astype(jnp.bfloat16)
+        reach = jnp.minimum(reach + jnp.dot(half, half, preferred_element_type=jnp.float32), 1.0)
+    pick_row = lax.broadcasted_iota(jnp.int32, (TREE_TOKENS, cols), 0)
+    pick_col = lax.broadcasted_iota(jnp.int32, (TREE_TOKENS, cols), 1)
+    pick = jnp.where(pick_row == x * rows + lax.rem(pick_col, rows), 1.0, 0.0)
+    usable = (
+        jnp.dot(
+            reach.astype(jnp.bfloat16),
+            pick.astype(jnp.bfloat16),
+            preferred_element_type=jnp.float32,
+        )
+        > 0.5
+    )
+
+    def stacked(slot, group):
+        first = group * heads * HEAD_SIZE
+        return [
+            gq[slot, :, first + h * HEAD_SIZE : first + (h + 1) * HEAD_SIZE] for h in range(heads)
+        ]
+
+    def softmax_part(key_rows, value_rows, query_rows, mask):
+        scores = (
+            lax.dot_general(
+                key_rows, query_rows, (((1,), (1,)), ((), ())), preferred_element_type=jnp.float32
+            )
+            * scale
+        )
+        scores = jnp.where(mask, scores, -1e30)
+        peak = jnp.maximum(jnp.max(scores, axis=0, keepdims=True), ABSENT)
+        w = jnp.exp2(scores - peak)
+        total = jnp.sum(w, axis=0, keepdims=True)
+        out = lax.dot_general(
+            value_rows,
+            w.astype(jnp.bfloat16),
+            (((0,), (0,)), ((), ())),
+            preferred_element_type=jnp.float32,
+        )
+        return out, peak, total
+
+    position = lax.broadcasted_iota(jnp.int32, (block_len, 2 * cols), 0) + blk * block_len
+
+    def cache_step(step):
+        request = z_back(step)
+        mask = position < len_ref[request]
+        for g in range(groups):
+            lanes = slice(g * HEAD_SIZE, (g + 1) * HEAD_SIZE)
+            query_rows = jnp.concatenate(
+                stacked(request * 2 + x, g) + stacked(request * 2 + other, g), axis=0
+            )
+            out, peak, total = softmax_part(
+                keys[request, :, lanes], values[request, :, lanes], query_rows, mask
+            )
+            own_o[step, g] = out[:, :cols]
+            xs_o[step, g] = out[:, cols:].astype(jnp.bfloat16)
+            for k, stat in enumerate((peak, total, peak, total)):
+                own_st[step, 4 * g + k : 4 * g + k + 1, :] = stat[:, :cols]
+                xs_st[step, 4 * g + k : 4 * g + k + 1, :] = stat[:, cols:]
+        for copy in x_copies(step):
+            copy.start()
+
+    def x_copies(step):
+        return (
+            remote(xs_o.at[step], xr_o.at[step], x_send.at[step, 0], x_recv.at[step, 0], partner),
+            remote(
+                xs_st.at[step], xr_st.at[step], x_send.at[step, 1], x_recv.at[step, 1], partner
+            ),
+        )
+
+    def z_copies(step):
+        device = (kv, z_back(step) * 2 + x)
+        return (
+            remote(zs_o.at[step], zr_o.at[step], z_send.at[step, 0], z_recv.at[step, 0], device),
+            remote(zs_st.at[step], zr_st.at[step], z_send.at[step, 1], z_recv.at[step, 1], device),
+        )
+
+    def combine(parts):
+        peak = parts[0][1]
+        for part in parts[1:]:
+            peak = jnp.maximum(peak, part[1])
+        out = total = None
+        for part_out, part_peak, part_total in parts:
+            factor = jnp.exp2(part_peak - peak)
+            out = part_out * factor if out is None else out + part_out * factor
+            total = part_total * factor if total is None else total + part_total * factor
+        return out, peak, total
+
+    def merge_step(step):
+        for copy in x_copies(step):
+            copy.wait_recv()
+        for g in range(groups):
+            out, peak, total = combine(
+                [
+                    (own_o[step, g], own_st[step, 4 * g : 4 * g + 1, :], own_st[step, 4 * g + 1 : 4 * g + 2, :]),
+                    (
+                        xr_o[step, g].astype(jnp.float32),
+                        xr_st[step, 4 * g : 4 * g + 1, :],
+                        xr_st[step, 4 * g + 1 : 4 * g + 2, :],
+                    ),
+                ]
+            )
+            if step == 0:
+                own_o[0, g] = out
+                own_st[0, 4 * g : 4 * g + 1, :] = peak
+                own_st[0, 4 * g + 1 : 4 * g + 2, :] = total
+            else:
+                zs_o[step, g] = out.astype(jnp.bfloat16)
+                for k, stat in enumerate((peak, total, peak, total)):
+                    zs_st[step, 4 * g + k : 4 * g + k + 1, :] = stat
+        if step:
+            for copy in z_copies(step):
+                copy.start()
+
+    load_keys.wait()
+    load_values.wait()
+    gather_forward(gq, 1, gz_send, gz_recv, gx_send, gx_recv)
+    gather_wait(gq, 0, gx_send, gx_recv)
+    draft_parts = []
+    for g in range(groups):
+        first = width_q + g * HEAD_SIZE
+        tree = gq[pl.ds(z * 2, 2), :, first : first + HEAD_SIZE].reshape(TREE_TOKENS, HEAD_SIZE)
+        first += width_kv
+        tree_v = gq[pl.ds(z * 2, 2), :, first : first + HEAD_SIZE].reshape(TREE_TOKENS, HEAD_SIZE)
+        query_rows = jnp.concatenate(stacked(blk, g), axis=0)
+        draft_parts.append(softmax_part(tree, tree_v, query_rows, usable))
+    for step in range(2, z_count):
+        gather_forward(gq, step, gz_send, gz_recv, gx_send, gx_recv)
+    order = list(range(1, z_count)) + [0]
+    previous = None
+    for step in order:
+        if step:
+            gather_wait(gq, step, gx_send, gx_recv)
+        cache_step(step)
+        if previous is not None:
+            merge_step(previous)
+        previous = step
+    merge_step(previous)
+
+    update_row = lax.broadcasted_iota(jnp.int32, (block_len, TREE_TOKENS), 0) + blk * block_len
+    update_col = lax.broadcasted_iota(jnp.int32, (block_len, TREE_TOKENS), 1)
+    update_wide = lax.broadcasted_iota(jnp.int32, (block_len, width_kv), 0) + blk * block_len
+    for r in range(requests):
+        length = len_ref[r]
+        accepted = count_ref[r]
+        offset = update_row - length
+        node = jnp.full((block_len, TREE_TOKENS), -1, jnp.int32)
+        for k in range(ACC):
+            node = jnp.where(offset == k, nodes_ref[r, k], node)
+        one_hot = jnp.where((node == update_col) & (offset < accepted), 1.0, 0.0).astype(
+            jnp.bfloat16
+        )
+        wide = update_wide - length
+        written = (wide >= 0) & (wide < accepted)
+        for cache, first in ((keys, width_q), (values, width_q + width_kv)):
+            tree = gq[2 * r : 2 * r + 2, :, first : first + width_kv].reshape(
+                TREE_TOKENS, width_kv
+            )
+            placed = jnp.dot(one_hot, tree, preferred_element_type=jnp.float32)
+            cache[r] = jnp.where(written, placed, cache[r].astype(jnp.float32)).astype(
+                jnp.bfloat16
+            )
+    store_keys = pltpu.make_async_copy(keys, new_key_hbm, local_sem.at[3])
+    store_values = pltpu.make_async_copy(values, new_value_hbm, local_sem.at[4])
+    store_keys.start()
+    store_values.start()
+
+    for step in range(1, z_count):
+        for copy in z_copies(step):
+            copy.wait_recv()
+    for g in range(groups):
+        low, high = 4 * g, 4 * g + 1
+        parts = [draft_parts[g], (own_o[0, g], own_st[0, low : low + 1, :], own_st[0, high : high + 1, :])]
+        for step in range(1, z_count):
+            parts.append(
+                (
+                    zr_o[step, g].astype(jnp.float32),
+                    zr_st[step, low : low + 1, :],
+                    zr_st[step, high : high + 1, :],
+                )
+            )
+        out, _, total = combine(parts)
+        turned = (out / total).T.astype(jnp.bfloat16)
+        for h in range(heads):
+            first = (g * heads + h) * HEAD_SIZE
+            ag[blk, :, first : first + HEAD_SIZE] = turned[h * rows : (h + 1) * rows, :]
+
+    gather_start(ag, az_send, az_recv, ax_send, ax_recv)
+    load_weight.wait()
+
+    def kv_copy(row_block, source):
+        return remote(
+            rs_send.at[row_block],
+            rs_recv.at[source],
+            r_send.at[row_block],
+            r_recv.at[source],
+            (row_block, blk),
+        )
+
+    def project(step):
+        row_block = z_back(step)
+        lhs = ag[pl.ds(row_block * 2, 2)].reshape(2 * rows, width_q)
+        part = jnp.dot(lhs, weight[...], preferred_element_type=jnp.float32)
+
+        @pl.when(row_block == kv)
+        def _():
+            out_ref[...] = part
+
+        @pl.when(row_block != kv)
+        def _():
+            rs_send[row_block] = part.astype(jnp.bfloat16)
+            kv_copy(row_block, kv).start()
+
+    gather_wait(ag, 0, ax_send, ax_recv)
+    gather_forward(ag, 1, az_send, az_recv, ax_send, ax_recv)
+    project(0)
+    for step in range(2, z_count):
+        gather_forward(ag, step, az_send, az_recv, ax_send, ax_recv)
+    for step in range(1, z_count):
+        gather_wait(ag, step, ax_send, ax_recv)
+        project(step)
+
+    gather_drain(gq, gz_send, gz_recv, gx_send, gx_recv)
+    gather_drain(ag, az_send, az_recv, ax_send, ax_recv)
+    for step in range(z_count):
+        for copy in x_copies(step):
+            copy.wait_send()
+        if step:
+            for copy in z_copies(step):
+                copy.wait_send()
+    store_keys.wait()
+    store_values.wait()
+    for step in range(1, kv_count):
+        peer = lax.rem(kv + step, kv_count)
+        copy = kv_copy(peer, peer)
+        copy.wait_recv()
+        out_ref[...] += rs_recv[peer].astype(jnp.float32)
+        copy.wait_send()
+
+
+def fused(
+    queries,
+    draft_token_keys,
+    draft_token_values,
+    cached_key_vectors,
+    cached_value_vectors,
+    out_weight,
+    lengths,
+    parents,
+    accepted_nodes,
+    accepted_count,
+):
+    blk_count = lax.axis_size("blk")
+    kv_count = lax.axis_size("kv")
+    z_count = blk_count // 2
+    rows, width_q = queries.shape
+    width_kv = draft_token_keys.shape[1]
+    groups = width_kv // HEAD_SIZE
+    cols = rows * (width_q // width_kv)
+    out_cols = out_weight.shape[1]
+    out_rows = rows * blk_count // kv_count
+    bf16, f32 = jnp.bfloat16, jnp.float32
+    outs = pltpu.VMEM((z_count, groups, HEAD_SIZE, cols), bf16)
+    stats = pltpu.VMEM((z_count, 4 * groups, cols), f32)
+    smem = pl.BlockSpec(memory_space=pltpu.SMEM)
+    vmem = pl.BlockSpec(memory_space=pltpu.VMEM)
+    anywhere = pl.BlockSpec(memory_space=pl.ANY)
+    dma = pltpu.SemaphoreType.DMA
+    projected, new_keys, new_values = pl.pallas_call(
+        functools.partial(fused_kernel, z_count, kv_count),
+        out_shape=(
+            jax.ShapeDtypeStruct((out_rows, out_cols), f32),
+            jax.ShapeDtypeStruct(cached_key_vectors.shape, bf16),
+            jax.ShapeDtypeStruct(cached_value_vectors.shape, bf16),
+        ),
+        in_specs=[smem] * 3 + [vmem] * 4 + [anywhere] * 3,
+        out_specs=(vmem, anywhere, anywhere),
+        scratch_shapes=[
+            pltpu.VMEM((blk_count, rows, width_q + 2 * width_kv), bf16),
+            pltpu.VMEM(cached_key_vectors.shape, bf16),
+            pltpu.VMEM(cached_value_vectors.shape, bf16),
+            pltpu.VMEM(out_weight.shape, bf16),
+            pltpu.VMEM((z_count, groups, HEAD_SIZE, cols), f32),
+            stats,
+            outs,
+            stats,
+            outs,
+            stats,
+            outs,
+            stats,
+            outs,
+            stats,
+            pltpu.VMEM((blk_count, rows, width_q), bf16),
+            pltpu.VMEM((kv_count, out_rows, out_cols), bf16),
+            pltpu.VMEM((kv_count, out_rows, out_cols), bf16),
+            dma((5,)),
+        ]
+        + [dma((z_count,))] * 4
+        + [dma((z_count, 2))] * 4
+        + [dma((z_count,))] * 4
+        + [dma((kv_count,))] * 2,
+        compiler_params=pltpu.CompilerParams(
+            collective_id=0, has_side_effects=True, vmem_limit_bytes=48 * 1024 * 1024
+        ),
+        cost_estimate=pl.CostEstimate(
+            flops=4 * 10**9, bytes_accessed=9 * 10**6, transcendentals=2 * 10**6
+        ),
+    )(
+        lengths,
+        accepted_count,
+        accepted_nodes,
+        parents,
+        queries,
+        draft_token_keys,
+        draft_token_values,
+        cached_key_vectors,
+        cached_value_vectors,
+        out_weight,
+    )
+    return (projected.astype(bf16), new_keys, new_values)
+
+
 def solution(mesh):
+    kv_count, blk_count = mesh.shape["kv"], mesh.shape["blk"]
+    paired = kv_count * 2 == blk_count and kv_count <= 4
     return jax.shard_map(
-        on_device,
+        fused if paired else on_device,
         mesh=mesh,
         in_specs=(
             P("blk", "kv"),

time: 212 us -> 78.8 us (0.37)
  waiting for transfers between devices: 75.1 us -> 0 us
  Pallas kernels: 0 us -> 67.7 us
  blocking collectives: 50.8 us -> 0 us
  matrix products: 19.6 us -> 0 us
  other arithmetic: 16.7 us -> 0.67 us
  starting transfers between devices: 15.9 us -> 0 us
  between operations: 14.1 us -> 0.66 us
  local copies, waits for them, and re-layouts: 18.6 us -> 9.39 us
    pallas_call x0 -> x1, Pallas kernels: none -> 67.7 us  [fused(): pl.pallas_call(functools.partial(fused_kernel, z_count, kv_count), out_sh...]
    all_gather x2 -> x0, waiting for transfers between devices: 53.2 us -> none  [the longest x1 53.2 us: on_device(): every_row = lax.all_gather(attention, 'blk', axis=0, tiled=True)]
    all_gather x2 -> x0, blocking collectives: 50.8 us -> none  [the longest x1 26 us: on_device(): lax.all_gather(draft_token_keys, 'blk', axis=0, tiled=True)]
    reduce_scatter x1 -> x0, waiting for transfers between devices: 20 us -> none  [on_device(): lax.psum_scatter(jnp.dot(every_row, out_weight, preferred_element_type=jn...]
    dot_general x13 -> x0, matrix products: 19.6 us -> none  [the longest x2 5.68 us: partial_softmax(): jnp.einsum('brkgtp,rbpkh->brtkgh', weights.astype(jnp.bfloat16), value_ro...]
    all_to_all x3 -> x0, starting transfers between devices: 15.7 us -> none  [the longest x1 5.44 us: on_device(): lax.all_to_all(local_out[0].astype(jnp.bfloat16), 'blk', split_axis=0, co...]
    reduce_sum x5 -> x0, other arithmetic: 8.48 us -> none  [the longest x2 5.52 us: partial_softmax(): weight_sum = jnp.sum(weights, axis=-1)]
    unnamed x18 -> x20, local copies, waits for them, and re-layouts: 4.62 us -> 9.39 us
  transfers between devices with their start and end apart: 6 -> 0, of which waited for: 3 -> 0; matrix products, arithmetic and copies ran while one was open for 17% -> 0% of each run, Pallas kernels for 0% -> 0%
where the time goes in v1:
time: 78.8 us; the launch traced here: 78.4 us
  Pallas kernels  67.7 us (86%)
  local copies, waits for them, and re-layouts  9.39 us (12%)
    pallas_call x1, Pallas kernels, fused(): pl.pallas_call(functools.partial(fused_kernel, z_count, kv_count), out_sh...  67.7 us
    unnamed x20, local copies, waits for them, and re-layouts  9.39 us

profile of v1, /device:TPU:1, one launch (start us, length us, event | category | flops | bytes accessed | tf_op | source)
XLA Modules:
  0.0 78.4 jit_solution(8749986453849019718)
XLA Ops:
  0.6 0.0 copy-start
  0.6 1.2 %copy-done = bf16[4,512,256]{2,1,0:T(8,128)(2,1)S(1)} copy-done((bf16[4,512,256]{2,1,0:T(8,128)(2,1)S(1)}, bf16[4,512,256]{2,1,0:T(8,128)(2,1)}, u32[]{:S(2)}) %copy-start) | copy-done | bytes 1048600
  1.9 0.0 copy-start.1
  1.9 1.2 %copy-done.1 = bf16[4,512,256]{2,1,0:T(8,128)(2,1)S(1)} copy-done((bf16[4,512,256]{2,1,0:T(8,128)(2,1)S(1)}, bf16[4,512,256]{2,1,0:T(8,128)(2,1)}, u32[]{:S(2)}) %copy-start.1) | copy-done | bytes 1048600
  3.1 0.0 copy-start.2
  3.1 0.9 %copy-done.2 = bf16[32,2048]{1,0:T(8,128)(2,1)S(1)} copy-done((bf16[32,2048]{1,0:T(8,128)(2,1)S(1)}, bf16[32,2048]{1,0:T(8,128)(2,1)}, u32[]{:S(2)}) %copy-start.2) | copy-done | bytes 131096
  4.0 0.0 copy-start.3
  4.0 0.7 copy-done.3
  4.7 0.0 copy-start.4
  4.7 0.7 copy-done.4
  5.4 0.0 copy-start.5
  5.4 0.7 copy-done.5
  6.1 0.0 copy-start.6
  6.1 0.7 copy-done.6
  6.8 0.0 copy-start.7
  6.8 0.7 copy-done.7
  7.4 0.0 copy-start.8
  7.4 0.7 copy-done.8
  8.1 67.7 %shard_map.121 = (f32[64,1024]{1,0:T(8,128)S(1)}, bf16[4,512,256]{2,1,0:T(8,128)(2,1)S(1)}, bf16[4,512,256]{2,1,0:T(8,128)(2,1)S(1)}) custom-call(s32[4]{0:T(128)S(1)} %copy-done.7, s32[4]{0:T(128)S(1)} %copy-done.8, s32[4,8]{1,0:T(4,128)S(1)} %copy-done.5, s32[4,64]{1,0:T(4,128)S(1)} %copy-done.6, bf16[32,2048]{1,0:T(8,128)(2,1)S(1)} %copy-done.2, ...), custom_call_target="tpu_custom_call" | custom-call | flops 4000000000 | bytes 9000000 | tf_op jit(solution)/shard_map/pallas_call | solution.py:592
  75.8 0.7 convert_element_type.3
  76.5 1.0 %copy.15 = bf16[4,512,256]{2,1,0:T(8,128)(2,1)} copy(bf16[4,512,256]{2,1,0:T(8,128)(2,1)S(1)} %get-tuple-element.13) | data formatting | bytes 2097152
  77.4 1.0 %copy.16 = bf16[4,512,256]{2,1,0:T(8,128)(2,1)} copy(bf16[4,512,256]{2,1,0:T(8,128)(2,1)S(1)} %get-tuple-element.14) | data formatting | bytes 2097152
Async XLA Ops:
  0.6 1.2 %copy-start = (bf16[4,512,256]{2,1,0:T(8,128)(2,1)S(1)}, bf16[4,512,256]{2,1,0:T(8,128)(2,1)}, u32[]{:S(2)}) copy-start(bf16[4,512,256]{2,1,0:T(8,128)(2,1)} %key_hbm.1) | copy-start | bytes 3145732
  1.9 1.2 %copy-start.1 = (bf16[4,512,256]{2,1,0:T(8,128)(2,1)S(1)}, bf16[4,512,256]{2,1,0:T(8,128)(2,1)}, u32[]{:S(2)}) copy-start(bf16[4,512,256]{2,1,0:T(8,128)(2,1)} %value_hbm.1) | copy-start | bytes 3145732
  3.1 0.9 %copy-start.2 = (bf16[32,2048]{1,0:T(8,128)(2,1)S(1)}, bf16[32,2048]{1,0:T(8,128)(2,1)}, u32[]{:S(2)}) copy-start(bf16[32,2048]{1,0:T(8,128)(2,1)} %q_ref.1) | copy-start | bytes 393220
  4.0 0.7 copy-start.3
  4.7 0.7 copy-start.4
  5.4 0.7 copy-start.5
  6.1 0.7 copy-start.6
  6.8 0.7 copy-start.7
  7.4 0.7 copy-start.8

commit v2 on v1

--- a/solution.py
+++ b/solution.py
@@ -193,20 +193,26 @@
 def fused_kernel(
     z_count,
     kv_count,
-    len_ref,
-    count_ref,
-    nodes_ref,
-    parents_ref,
-    q_ref,
-    dk_ref,
-    dv_ref,
+    len_hbm,
+    count_hbm,
+    nodes_hbm,
+    parents_hbm,
+    q_hbm,
+    dk_hbm,
+    dv_hbm,
     key_hbm,
     value_hbm,
     weight_hbm,
     out_ref,
     new_key_hbm,
     new_value_hbm,
+    len_ref,
+    count_ref,
+    nodes_ref,
+    parents_ref,
     gq,
+    tree,
+    picked,
     keys,
     values,
     weight,
@@ -228,6 +234,10 @@
     gz_recv,
     gx_send,
     gx_recv,
+    t_send,
+    t_recv,
+    p_send,
+    p_recv,
     x_send,
     x_recv,
     z_send,
@@ -245,8 +255,8 @@
     x = blk % 2
     other = 1 - x
     partner = (kv, z * 2 + other)
-    rows, width_q = q_ref.shape
-    width_kv = dk_ref.shape[1]
+    rows, width_q = q_hbm.shape
+    width_kv = dk_hbm.shape[1]
     groups = width_kv // HEAD_SIZE
     heads = width_q // width_kv
     cols = rows * heads
@@ -262,13 +272,25 @@
     load_keys = pltpu.make_async_copy(key_hbm, keys, local_sem.at[0])
     load_values = pltpu.make_async_copy(value_hbm, values, local_sem.at[1])
     load_weight = pltpu.make_async_copy(weight_hbm, weight, local_sem.at[2])
+    first_loads = [
+        pltpu.make_async_copy(src, dst, local_sem.at[5 + i])
+        for i, (src, dst) in enumerate(
+            (
+                (q_hbm, gq.at[blk]),
+                (dk_hbm, tree.at[0, x]),
+                (dv_hbm, tree.at[1, x]),
+                (parents_hbm, parents_ref),
+                (nodes_hbm, nodes_ref),
+                (len_hbm, len_ref),
+                (count_hbm, count_ref),
+            )
+        )
+    ]
+    for load in first_loads:
+        load.start()
     load_keys.start()
     load_values.start()
     load_weight.start()
-
-    gq[blk, :, 0:width_q] = q_ref[...]
-    gq[blk, :, width_q : width_q + width_kv] = dk_ref[...]
-    gq[blk, :, width_q + width_kv :] = dv_ref[...]
 
     barrier = pltpu.get_barrier_semaphore()
     pl.semaphore_signal(barrier, inc=1, device_id=partner, device_id_type=MESH_ID)
@@ -314,7 +336,21 @@
             if step:
                 remote(here, here, zs.at[step], zr.at[step], partner).wait_send()
 
+    def tree_copy(which):
+        own = tree.at[which, x]
+        return remote(own, own, t_send.at[which], t_recv.at[which], partner)
+
+    def picked_copy(step):
+        own = picked.at[z]
+        return remote(own, own, p_send.at[step], p_recv.at[step], (kv, z_at(step) * 2 + x))
+
+    for load in first_loads[:3]:
+        load.wait()
     gather_start(gq, gz_send, gz_recv, gx_send, gx_recv)
+    for which in range(2):
+        tree_copy(which).start()
+    for load in first_loads[3:]:
+        load.wait()
 
     node_row = lax.broadcasted_iota(jnp.int32, (TREE_TOKENS, TREE_TOKENS), 0)
     node_col = lax.broadcasted_iota(jnp.int32, (TREE_TOKENS, TREE_TOKENS), 1)
@@ -439,14 +475,34 @@
     load_values.wait()
     gather_forward(gq, 1, gz_send, gz_recv, gx_send, gx_recv)
     gather_wait(gq, 0, gx_send, gx_recv)
+    for which in range(2):
+        tree_copy(which).wait_recv()
+    slot_row = lax.broadcasted_iota(jnp.int32, (ACC, TREE_TOKENS), 0)
+    slot_col = lax.broadcasted_iota(jnp.int32, (ACC, TREE_TOKENS), 1)
+    node = jnp.zeros((ACC, TREE_TOKENS), jnp.int32)
+    for k in range(ACC):
+        node = jnp.where(slot_row == k, nodes_ref[z, k], node)
+    one_hot = jnp.where(node == slot_col, 1.0, 0.0).astype(jnp.bfloat16)
+    picked[z] = jnp.concatenate(
+        [
+            jnp.dot(
+                one_hot,
+                tree[which].reshape(TREE_TOKENS, width_kv),
+                preferred_element_type=jnp.float32,
+            )
+            for which in range(2)
+        ],
+        axis=0,
+    ).astype(jnp.bfloat16)
+    for step in range(1, z_count):
+        picked_copy(step).start()
     draft_parts = []
     for g in range(groups):
-        first = width_q + g * HEAD_SIZE
-        tree = gq[pl.ds(z * 2, 2), :, first : first + HEAD_SIZE].reshape(TREE_TOKENS, HEAD_SIZE)
-        first += width_kv
-        tree_v = gq[pl.ds(z * 2, 2), :, first : first + HEAD_SIZE].reshape(TREE_TOKENS, HEAD_SIZE)
+        lanes = slice(g * HEAD_SIZE, (g + 1) * HEAD_SIZE)
+        tree_k = tree[0, :, :, lanes].reshape(TREE_TOKENS, HEAD_SIZE)
+        tree_v = tree[1, :, :, lanes].reshape(TREE_TOKENS, HEAD_SIZE)
         query_rows = jnp.concatenate(stacked(blk, g), axis=0)
-        draft_parts.append(softmax_part(tree, tree_v, query_rows, usable))
+        draft_parts.append(softmax_part(tree_k, tree_v, query_rows, usable))
     for step in range(2, z_count):
         gather_forward(gq, step, gz_send, gz_recv, gx_send, gx_recv)
     order = list(range(1, z_count)) + [0]
@@ -460,26 +516,22 @@
         previous = step
     merge_step(previous)
 
-    update_row = lax.broadcasted_iota(jnp.int32, (block_len, TREE_TOKENS), 0) + blk * block_len
-    update_col = lax.broadcasted_iota(jnp.int32, (block_len, TREE_TOKENS), 1)
+    for step in range(1, z_count):
+        picked_copy(step).wait_recv()
+    update_row = lax.broadcasted_iota(jnp.int32, (block_len, 2 * ACC), 0) + blk * block_len
+    update_col = lax.broadcasted_iota(jnp.int32, (block_len, 2 * ACC), 1)
     update_wide = lax.broadcasted_iota(jnp.int32, (block_len, width_kv), 0) + blk * block_len
     for r in range(requests):
-        length = len_ref[r]
-        accepted = count_ref[r]
-        offset = update_row - length
-        node = jnp.full((block_len, TREE_TOKENS), -1, jnp.int32)
-        for k in range(ACC):
-            node = jnp.where(offset == k, nodes_ref[r, k], node)
-        one_hot = jnp.where((node == update_col) & (offset < accepted), 1.0, 0.0).astype(
-            jnp.bfloat16
-        )
-        wide = update_wide - length
-        written = (wide >= 0) & (wide < accepted)
-        for cache, first in ((keys, width_q), (values, width_q + width_kv)):
-            tree = gq[2 * r : 2 * r + 2, :, first : first + width_kv].reshape(
-                TREE_TOKENS, width_kv
-            )
-            placed = jnp.dot(one_hot, tree, preferred_element_type=jnp.float32)
+        wide = update_wide - len_ref[r]
+        written = (wide >= 0) & (wide < count_ref[r])
+        for which, cache in enumerate((keys, values)):
+            offset = update_row - len_ref[r]
+            one_hot = jnp.where(
+                (offset + which * ACC == update_col) & (offset >= 0) & (offset < ACC), 1.0, 0.0
+            )
+            placed = jnp.dot(
+                one_hot.astype(jnp.bfloat16), picked[r], preferred_element_type=jnp.float32
+            )
             cache[r] = jnp.where(written, placed, cache[r].astype(jnp.float32)).astype(
                 jnp.bfloat16
             )
@@ -551,6 +603,10 @@
         if step:
             for copy in z_copies(step):
                 copy.wait_send()
+    for which in range(2):
+        tree_copy(which).wait_send()
+    for step in range(1, z_count):
+        picked_copy(step).wait_send()
     store_keys.wait()
     store_values.wait()
     for step in range(1, kv_count):
@@ -585,9 +641,8 @@
     bf16, f32 = jnp.bfloat16, jnp.float32
     outs = pltpu.VMEM((z_count, groups, HEAD_SIZE, cols), bf16)
     stats = pltpu.VMEM((z_count, 4 * groups, cols), f32)
-    smem = pl.BlockSpec(memory_space=pltpu.SMEM)
     vmem = pl.BlockSpec(memory_space=pltpu.VMEM)
-    anywhere = pl.BlockSpec(memory_space=pl.ANY)
+    hbm = pl.BlockSpec(memory_space=pltpu.HBM)
     dma = pltpu.SemaphoreType.DMA
     projected, new_keys, new_values = pl.pallas_call(
         functools.partial(fused_kernel, z_count, kv_count),
@@ -596,10 +651,16 @@
             jax.ShapeDtypeStruct(cached_key_vectors.shape, bf16),
             jax.ShapeDtypeStruct(cached_value_vectors.shape, bf16),
         ),
-        in_specs=[smem] * 3 + [vmem] * 4 + [anywhere] * 3,
-        out_specs=(vmem, anywhere, anywhere),
+        in_specs=[hbm] * 10,
+        out_specs=(vmem, hbm, hbm),
         scratch_shapes=[
-            pltpu.VMEM((blk_count, rows, width_q + 2 * width_kv), bf16),
+            pltpu.SMEM(lengths.shape, jnp.int32),
+            pltpu.SMEM(accepted_count.shape, jnp.int32),
+            pltpu.SMEM(accepted_nodes.shape, jnp.int32),
+            pltpu.VMEM(parents.shape, jnp.int32),
+            pltpu.VMEM((blk_count, rows, width_q), bf16),
+            pltpu.VMEM((2, 2, rows, width_kv), bf16),
+            pltpu.VMEM((z_count, 2 * ACC, width_kv), bf16),
             pltpu.VMEM(cached_key_vectors.shape, bf16),
             pltpu.VMEM(cached_value_vectors.shape, bf16),
             pltpu.VMEM(out_weight.shape, bf16),
@@ -616,14 +677,16 @@
             pltpu.VMEM((blk_count, rows, width_q), bf16),
             pltpu.VMEM((kv_count, out_rows, out_cols), bf16),
             pltpu.VMEM((kv_count, out_rows, out_cols), bf16),
-            dma((5,)),
+            dma((12,)),
         ]
         + [dma((z_count,))] * 4
+        + [dma((2,))] * 2
+        + [dma((z_count,))] * 2
         + [dma((z_count, 2))] * 4
         + [dma((z_count,))] * 4
         + [dma((kv_count,))] * 2,
         compiler_params=pltpu.CompilerParams(
-            collective_id=0, has_side_effects=True, vmem_limit_bytes=48 * 1024 * 1024
+            collective_id=0, has_side_effects=True, vmem_limit_bytes=63 * 1024 * 1024
         ),
         cost_estimate=pl.CostEstimate(
             flops=4 * 10**9, bytes_accessed=9 * 10**6, transcendentals=2 * 10**6

time: 78.8 us -> 70.4 us (0.89)
  local copies, waits for them, and re-layouts: 9.39 us -> 4.52 us
  Pallas kernels: 67.7 us -> 63.4 us
  other arithmetic: 0.67 us -> 1.62 us
    unnamed x20 -> x2, local copies, waits for them, and re-layouts: 9.39 us -> 4.52 us
    pallas_call x1, Pallas kernels: 67.7 us -> 63.4 us  [fused(): pl.pallas_call(functools.partial(fused_kernel, z_count, kv_count), out_sh...]
    convert_element_type x1, other arithmetic: 0.67 us -> 1.62 us  [fused(): return (projected.astype(bf16), new_keys, new_values)]
where the time goes in v2:
time: 70.4 us; the launch traced here: 70.2 us
  Pallas kernels  63.4 us (90%)
  local copies, waits for them, and re-layouts  4.52 us (6%)
  other arithmetic  1.62 us (2%)
    pallas_call x1, Pallas kernels, fused(): pl.pallas_call(functools.partial(fused_kernel, z_count, kv_count), out_sh...  63.4 us
    unnamed x2, local copies, waits for them, and re-layouts  4.52 us
    convert_element_type x1, other arithmetic, fused(): return (projected.astype(bf16), new_keys, new_values)  1.62 us

profile of v2, /device:TPU:1, one launch (start us, length us, event | category | flops | bytes accessed | tf_op | source)
XLA Modules:
  0.0 70.2 jit_solution(13764619478537246594)
XLA Ops:
  0.6 63.4 %shard_map.121 = (f32[64,1024]{1,0:T(8,128)}, bf16[4,512,256]{2,1,0:T(8,128)(2,1)}, bf16[4,512,256]{2,1,0:T(8,128)(2,1)}) custom-call(s32[4]{0:T(128)} %len_hbm.1, s32[4]{0:T(128)} %count_hbm.1, s32[4,8]{1,0:T(4,128)} %nodes_hbm.1, s32[4,64]{1,0:T(4,128)} %parents_hbm.1, bf16[32,2048]{1,0:T(8,128)(2,1)} %q_hbm.1, bf16[32,256]{1,0:T(8,128)(2,1)} %dk_hbm.1, ...), custom_call_target="tpu_custom_call" | custom-call | flops 4000000000 | bytes 9000000 | tf_op jit(solution)/shard_map/pallas_call | solution.py:647
  64.1 1.6 %convert_element_type.3 = bf16[64,1024]{1,0:T(8,128)(2,1)} convert(f32[64,1024]{1,0:T(8,128)} %get-tuple-element.6) | non-fusion elementwise | flops 65536 | bytes 393216 | tf_op jit(solution)/shard_map/convert_element_type | solution.py:706
  65.7 2.3 %copy.15 = bf16[4,512,256]{2,1,0:T(8,128)(2,1)} copy(bf16[4,512,256]{2,1,0:T(8,128)(2,1)} %get-tuple-element.13) | data formatting | bytes 2097152
  67.9 2.3 %copy.16 = bf16[4,512,256]{2,1,0:T(8,128)(2,1)} copy(bf16[4,512,256]{2,1,0:T(8,128)(2,1)} %get-tuple-element.14) | data formatting | bytes 2097152

commit v3 on v2

--- a/solution.py
+++ b/solution.py
@@ -188,6 +188,7 @@
 LOG2E = 1.4426950408889634
 MESH_ID = pl.DeviceIdType.MESH
 ABSENT = -1e20
+PARTS = 2
 
 
 def fused_kernel(
@@ -314,27 +315,37 @@
             device_id_type=MESH_ID,
         )
 
+    part_rows = rows // PARTS
+
+    def piece(buf, slot, part):
+        return buf.at[slot, pl.ds(part * part_rows, part_rows)]
+
     def gather_start(buf, zs, zr, xs, xr):
-        here = buf.at[blk]
-        remote(here, here, xs.at[0], xr.at[0], partner).start()
+        for part in range(PARTS):
+            here = piece(buf, blk, part)
+            remote(here, here, xs.at[0, part], xr.at[0, part], partner).start()
+            for step in range(1, z_count):
+                device = (kv, z_at(step) * 2 + x)
+                remote(here, here, zs.at[step, part], zr.at[step, part], device).start()
+
+    def gather_forward(buf, part, zs, zr, xs, xr):
         for step in range(1, z_count):
-            remote(here, here, zs.at[step], zr.at[step], (kv, z_at(step) * 2 + x)).start()
-
-    def gather_forward(buf, step, zs, zr, xs, xr):
-        slot = buf.at[z_back(step) * 2 + x]
-        remote(slot, slot, zs.at[step], zr.at[step], partner).wait_recv()
-        remote(slot, slot, xs.at[step], xr.at[step], partner).start()
+            here = piece(buf, z_back(step) * 2 + x, part)
+            remote(here, here, zs.at[step, part], zr.at[step, part], partner).wait_recv()
+            remote(here, here, xs.at[step, part], xr.at[step, part], partner).start()
 
     def gather_wait(buf, step, xs, xr):
-        slot = buf.at[z_back(step) * 2 + other]
-        remote(slot, slot, xs.at[step], xr.at[step], partner).wait_recv()
+        for part in range(PARTS):
+            here = piece(buf, z_back(step) * 2 + other, part)
+            remote(here, here, xs.at[step, part], xr.at[step, part], partner).wait_recv()
 
     def gather_drain(buf, zs, zr, xs, xr):
-        here = buf.at[blk]
-        for step in range(z_count):
-            remote(here, here, xs.at[step], xr.at[step], partner).wait_send()
-            if step:
-                remote(here, here, zs.at[step], zr.at[step], partner).wait_send()
+        for part in range(PARTS):
+            here = piece(buf, blk, part)
+            for step in range(z_count):
+                remote(here, here, xs.at[step, part], xr.at[step, part], partner).wait_send()
+                if step:
+                    remote(here, here, zs.at[step, part], zr.at[step, part], partner).wait_send()
 
     def tree_copy(which):
         own = tree.at[which, x]
@@ -473,8 +484,6 @@
 
     load_keys.wait()
     load_values.wait()
-    gather_forward(gq, 1, gz_send, gz_recv, gx_send, gx_recv)
-    gather_wait(gq, 0, gx_send, gx_recv)
     for which in range(2):
         tree_copy(which).wait_recv()
     slot_row = lax.broadcasted_iota(jnp.int32, (ACC, TREE_TOKENS), 0)
@@ -503,8 +512,9 @@
         tree_v = tree[1, :, :, lanes].reshape(TREE_TOKENS, HEAD_SIZE)
         query_rows = jnp.concatenate(stacked(blk, g), axis=0)
         draft_parts.append(softmax_part(tree_k, tree_v, query_rows, usable))
-    for step in range(2, z_count):
-        gather_forward(gq, step, gz_send, gz_recv, gx_send, gx_recv)
+    gather_wait(gq, 0, gx_send, gx_recv)
+    for part in range(PARTS):
+        gather_forward(gq, part, gz_send, gz_recv, gx_send, gx_recv)
     order = list(range(1, z_count)) + [0]
     previous = None
     for step in order:
@@ -587,10 +597,9 @@
             kv_copy(row_block, kv).start()
 
     gather_wait(ag, 0, ax_send, ax_recv)
-    gather_forward(ag, 1, az_send, az_recv, ax_send, ax_recv)
     project(0)
-    for step in range(2, z_count):
-        gather_forward(ag, step, az_send, az_recv, ax_send, ax_recv)
+    for part in range(PARTS):
+        gather_forward(ag, part, az_send, az_recv, ax_send, ax_recv)
     for step in range(1, z_count):
         gather_wait(ag, step, ax_send, ax_recv)
         project(step)
@@ -679,11 +688,11 @@
             pltpu.VMEM((kv_count, out_rows, out_cols), bf16),
             dma((12,)),
         ]
-        + [dma((z_count,))] * 4
+        + [dma((z_count, PARTS))] * 4
         + [dma((2,))] * 2
         + [dma((z_count,))] * 2
         + [dma((z_count, 2))] * 4
-        + [dma((z_count,))] * 4
+        + [dma((z_count, PARTS))] * 4
         + [dma((kv_count,))] * 2,
         compiler_params=pltpu.CompilerParams(
             collective_id=0, has_side_effects=True, vmem_limit_bytes=63 * 1024 * 1024

time: 70.4 us -> 69.5 us (0.987)
  Pallas kernels: 63.4 us -> 62.5 us
    pallas_call x1, Pallas kernels: 63.4 us -> 62.5 us  [fused(): pl.pallas_call(functools.partial(fused_kernel, z_count, kv_count), out_sh...]
where the time goes in v3:
time: 69.5 us; the launch traced here: 69.3 us
  Pallas kernels  62.5 us (90%)
  local copies, waits for them, and re-layouts  4.52 us (7%)
  other arithmetic  1.62 us (2%)
    pallas_call x1, Pallas kernels, fused(): pl.pallas_call(functools.partial(fused_kernel, z_count, kv_count), out_sh...  62.5 us
    unnamed x2, local copies, waits for them, and re-layouts  4.52 us
    convert_element_type x1, other arithmetic, fused(): return (projected.astype(bf16), new_keys, new_values)  1.62 us

profile of v3, /device:TPU:1, one launch (start us, length us, event | category | flops | bytes accessed | tf_op | source)
XLA Modules:
  0.0 69.3 jit_solution(7912810946348633914)
XLA Ops:
  0.6 62.5 %shard_map.121 = (f32[64,1024]{1,0:T(8,128)}, bf16[4,512,256]{2,1,0:T(8,128)(2,1)}, bf16[4,512,256]{2,1,0:T(8,128)(2,1)}) custom-call(s32[4]{0:T(128)} %len_hbm.1, s32[4]{0:T(128)} %count_hbm.1, s32[4,8]{1,0:T(4,128)} %nodes_hbm.1, s32[4,64]{1,0:T(4,128)} %parents_hbm.1, bf16[32,2048]{1,0:T(8,128)(2,1)} %q_hbm.1, bf16[32,256]{1,0:T(8,128)(2,1)} %dk_hbm.1, ...), custom_call_target="tpu_custom_call" | custom-call | flops 4000000000 | bytes 9000000 | tf_op jit(solution)/shard_map/pallas_call | solution.py:656
  63.2 1.6 %convert_element_type.3 = bf16[64,1024]{1,0:T(8,128)(2,1)} convert(f32[64,1024]{1,0:T(8,128)} %get-tuple-element.6) | non-fusion elementwise | flops 65536 | bytes 393216 | tf_op jit(solution)/shard_map/convert_element_type | solution.py:715
  64.8 2.3 %copy.15 = bf16[4,512,256]{2,1,0:T(8,128)(2,1)} copy(bf16[4,512,256]{2,1,0:T(8,128)(2,1)} %get-tuple-element.13) | data formatting | bytes 2097152
  67.1 2.3 %copy.16 = bf16[4,512,256]{2,1,0:T(8,128)(2,1)} copy(bf16[4,512,256]{2,1,0:T(8,128)(2,1)} %get-tuple-element.14) | data formatting | bytes 2097152

commit v4 on v3

--- a/solution.py
+++ b/solution.py
@@ -484,6 +484,8 @@
 
     load_keys.wait()
     load_values.wait()
+    gather_wait(gq, 0, gx_send, gx_recv)
+    cache_step(0)
     for which in range(2):
         tree_copy(which).wait_recv()
     slot_row = lax.broadcasted_iota(jnp.int32, (ACC, TREE_TOKENS), 0)
@@ -512,19 +514,15 @@
         tree_v = tree[1, :, :, lanes].reshape(TREE_TOKENS, HEAD_SIZE)
         query_rows = jnp.concatenate(stacked(blk, g), axis=0)
         draft_parts.append(softmax_part(tree_k, tree_v, query_rows, usable))
-    gather_wait(gq, 0, gx_send, gx_recv)
     for part in range(PARTS):
         gather_forward(gq, part, gz_send, gz_recv, gx_send, gx_recv)
-    order = list(range(1, z_count)) + [0]
-    previous = None
-    for step in order:
-        if step:
-            gather_wait(gq, step, gx_send, gx_recv)
+    merge_step(0)
+    for step in range(1, z_count):
+        gather_wait(gq, step, gx_send, gx_recv)
         cache_step(step)
-        if previous is not None:
-            merge_step(previous)
-        previous = step
-    merge_step(previous)
+        if step > 1:
+            merge_step(step - 1)
+    merge_step(z_count - 1)
 
     for step in range(1, z_count):
         picked_copy(step).wait_recv()

time: 69.5 us -> 70.9 us (1.020); the launches traced: 69.3 us -> 69.7 us
  no operation moved by 1% of the time
where the time goes in v4:
time: 70.9 us; the launch traced here: 69.7 us
  Pallas kernels  63 us (89%)
  local copies, waits for them, and re-layouts  4.52 us (6%)
  other arithmetic  1.62 us (2%)
    pallas_call x1, Pallas kernels, fused(): pl.pallas_call(functools.partial(fused_kernel, z_count, kv_count), out_sh...  63 us
    unnamed x2, local copies, waits for them, and re-layouts  4.52 us
    convert_element_type x1, other arithmetic, fused(): return (projected.astype(bf16), new_keys, new_values)  1.62 us

profile of v4, /device:TPU:1, one launch (start us, length us, event | category | flops | bytes accessed | tf_op | source)
XLA Modules:
  0.0 69.7 jit_solution(7411324748930214560)
XLA Ops:
  0.6 63.0 %shard_map.121 = (f32[64,1024]{1,0:T(8,128)}, bf16[4,512,256]{2,1,0:T(8,128)(2,1)}, bf16[4,512,256]{2,1,0:T(8,128)(2,1)}) custom-call(s32[4]{0:T(128)} %len_hbm.1, s32[4]{0:T(128)} %count_hbm.1, s32[4,8]{1,0:T(4,128)} %nodes_hbm.1, s32[4,64]{1,0:T(4,128)} %parents_hbm.1, bf16[32,2048]{1,0:T(8,128)(2,1)} %q_hbm.1, bf16[32,256]{1,0:T(8,128)(2,1)} %dk_hbm.1, ...), custom_call_target="tpu_custom_call" | custom-call | flops 4000000000 | bytes 9000000 | tf_op jit(solution)/shard_map/pallas_call | solution.py:654
  63.6 1.6 %convert_element_type.3 = bf16[64,1024]{1,0:T(8,128)(2,1)} convert(f32[64,1024]{1,0:T(8,128)} %get-tuple-element.6) | non-fusion elementwise | flops 65536 | bytes 393216 | tf_op jit(solution)/shard_map/convert_element_type | solution.py:713
  65.2 2.3 %copy.15 = bf16[4,512,256]{2,1,0:T(8,128)(2,1)} copy(bf16[4,512,256]{2,1,0:T(8,128)(2,1)} %get-tuple-element.13) | data formatting | bytes 2097152
  67.5 2.3 %copy.16 = bf16[4,512,256]{2,1,0:T(8,128)(2,1)} copy(bf16[4,512,256]{2,1,0:T(8,128)(2,1)} %get-tuple-element.14) | data formatting | bytes 2097152
